TPU v7x, 128 devices: a whole 4x4x4 slice. The times are simulated.
128 devices in a mesh: row: 16 (over x_lo, y, core), col: 8 (over z, x_hi).
Axes of the slice: x: 4 (x_hi: 2, x_lo: 2; x = x_hi * 2 + x_lo), y: 4, z: 4, core: 2. Of those that a mesh axis runs over, the one named last changes fastest.
Arguments:
- integrals: float32 [4096, 1024], P('row', 'col'), may hold values from -0.1875 to 0.1875
- amplitudes: float32 [10240, 4096], P('row', 'col'), may hold values from -6 to 6
Outputs:
- cycle_residual: float32 [4096, 40960], P('row', 'col')
All inputs are finite; a program needn't handle non-finite values.
Results may differ from a plain program's by a relative error of at most 0.00007.
Values sent between devices are 32-bit elements; how exact they have to be, the bound alone decides.
A program may use at most 128 MiB of HBM per device.

v0:
```python
import jax
import jax.numpy as jnp
from jax import lax
from jax.sharding import PartitionSpec as P

O = 64
V = 640
PANEL = 256
PANELS = 4


def broadcast(block, axis, holder):
    block = jnp.where(lax.axis_index(axis) == holder, block, jnp.zeros_like(block))
    return lax.psum(block, axis)


def per_device(integrals, amplitudes):
    local_pairs = amplitudes.shape[1] // O
    local_virt = amplitudes.shape[0] // V
    blocks = amplitudes.reshape(local_virt, V, local_pairs, O)
    moved = lax.all_to_all(blocks, "col", split_axis=1, concat_axis=2, tiled=True)
    outer_virt = moved.shape[1]
    cycle_local = jnp.transpose(moved, (0, 2, 1, 3)).reshape(local_virt * O, outer_virt * O)
    integral_width = integrals.shape[1]
    amplitude_height = cycle_local.shape[0]
    unit = min(integral_width, amplitude_height)
    total = jnp.zeros((integrals.shape[0], cycle_local.shape[1]), jnp.float32)
    for panel_index in range(PANELS):
        first = panel_index * PANEL
        integral_pieces = {}
        amplitude_pieces = {}
        for part_index in range(PANEL // integral_width):
            owner = first // integral_width + part_index
            integral_pieces[owner] = broadcast(integrals, "col", owner)
        for part_index in range(PANEL // amplitude_height):
            owner = first // amplitude_height + part_index
            amplitude_pieces[owner] = broadcast(cycle_local, "row", owner)
        for begin in range(first, first + PANEL, unit):
            left_piece = integral_pieces[begin // integral_width]
            left_offset = begin % integral_width
            right_piece = amplitude_pieces[begin // amplitude_height]
            right_offset = begin % amplitude_height
            total = total + jnp.dot(
                left_piece[:, left_offset : left_offset + unit],
                right_piece,
                precision=lax.Precision.HIGHEST,
                preferred_element_type=jnp.float32,
            )
    return total


def solution(mesh):
    placed = (P("row", "col"), P("row", "col"))
    return jax.shard_map(
        per_device, mesh=mesh, in_specs=placed, out_specs=P("row", "col"), check_vma=False
    )
```

profile of v0, /device:TPU:1, one launch (start us, length us, event | category | flops | bytes accessed | tf_op | source)
XLA Modules:
  0.0 519.4 jit_solution(2824282583526115950)
XLA Ops:
  6.5 2.8 copy.54
  14.1 8.5 %all-to-all-start = ((f32[8,1,40960]{2,1,0:T(1,128)}), f32[8,1,40960]{2,1,0:T(1,128)S(1)}, u32[]{:S(2)}, u32[]{:S(2)}) async-start(f32[8,1,40960]{2,1,0:T(1,128)} %reshape.149), calls=%async_computation | async-start | bytes 2621440 | tf_op jit(solution)/shard_map/all_to_all | solution.py:21
  23.8 17.9 %all-to-all-done = f32[8,1,40960]{2,1,0:T(1,128)S(1)} async-done(((f32[8,1,40960]{2,1,0:T(1,128)}), f32[8,1,40960]{2,1,0:T(1,128)S(1)}, u32[]{:S(2)}, u32[]{:S(2)}) %all-to-all-start) | async-done | bytes 1310752 | tf_op jit(solution)/shard_map/all_to_all | solution.py:21
  42.2 5.2 %reduce = f32[8,40960]{1,0:T(8,128)} reduce(f32[8,1,40960]{2,1,0:T(1,128)S(1)} %all-to-all-done, f32[]{:T(128)} %broadcast.338), dimensions={1}, to_apply=%all_to_all.4.reduce_sub_computation | reduce | bytes 2621444 | tf_op jit(solution)/shard_map/all_to_all | solution.py:21
  49.8 14.1 %broadcast_select_fusion = (f32[1,640,8,64]{3,2,0,1:T(8,128)}, f32[1,640,8,64]{3,2,0,1:T(8,128)}, f32[1,640,8,64]{3,2,0,1:T(8,128)}, f32[1,640,8,64]{3,2,0,1:T(8...) fusion(pred[]{:T(512)S(6)} %eq.95, pred[]{:T(512)S(6)} %eq.94, ...), kind=kLoop, calls=%fused_computation.15 | loop fusion | flops 5242880 | bytes 22282256 | tf_op jit(solution)/shard_map/jit(_where)/select_n | solution.py:13
  64.0 2.6 copy.104
  72.2 2.6 copy.105
  80.4 2.6 copy.106
  88.6 2.6 copy.107
  97.1 2.6 copy.108
  105.2 2.6 copy.109
  113.5 2.6 copy.110
  121.7 2.6 copy.111
  129.8 2.6 copy.112
  154.8 2.6 copy.115
  196.1 241.4 %all-reduce.5.cloned.1.call-done = (f32[64,5120]{1,0:T(8,128)}, f32[64,5120]{1,0:T(8,128)}, f32[64,5120]{1,0:T(8,128)}, f32[64,5120]{1,0:T(8,128)}, f32[64,5120]...) async-done(((f32[64,5120]{1,0:T(8,128)}, ...) | async-done | bytes 20971536 | tf_op jit(solution)/shard_map/psum | solution.py:14
  437.5 5.8 %fusion.15 = f32[256,5120]{1,0:T(8,128)S(1)} fusion(f32[64,5120]{1,0:T(8,128)} %get-tuple-element.5, f32[256,128]{1,0:T(8,128)} %get-tuple-element.21), kind=kOutput, calls=%fused_computation.46 | convolution fusion | flops 1006632960 | bytes 6684672 | tf_op jit(solution)/shard_map/dot_general | solution.py:43
  443.3 4.4 convolution_add_fusion.14
  447.7 4.5 convolution_add_fusion.13
  452.3 4.4 convolution_add_fusion.12
  456.7 4.3 convolution_add_fusion.11
  461.1 4.8 convolution_add_fusion.10
  465.9 4.3 convolution_add_fusion.9
  470.3 4.4 convolution_add_fusion.8
  474.7 4.5 convolution_add_fusion.7
  479.2 4.4 convolution_add_fusion.6
  483.6 4.3 convolution_add_fusion.5
  488.0 4.6 convolution_add_fusion.4
  492.6 4.3 convolution_add_fusion.3
  497.0 4.4 convolution_add_fusion.2
  501.4 4.6 convolution_add_fusion.1
  506.0 6.1 %convolution_add_fusion = f32[256,5120]{1,0:T(8,128)} fusion(f32[256,5120]{1,0:T(8,128)S(1)} %convolution_add_fusion.1, f32[64,5120]{1,0:T(8,128)S(1)} %copy-done, f32[256,128]{1,0:T(8,128)S(1)} %copy-done.15), kind=kOutput, calls=%fused_computation | convolution fusion | flops 1007943680 | bytes 11927552 | tf_op jit(solution)/shard_map/dot_general | solution.py:43
  (112 shorter events, 114.5 us)
Async XLA Ops:
  14.1 8.5 %copy-start.23 = (f32[256,128]{1,0:T(8,128)S(1)}, f32[256,128]{1,0:T(8,128)}, u32[]{:S(2)}) copy-start(f32[256,128]{1,0:T(8,128)} %param.2) | copy-start | bytes 393220
  14.1 27.6 %all-to-all-start = ((f32[8,1,40960]{2,1,0:T(1,128)}), f32[8,1,40960]{2,1,0:T(1,128)S(1)}, u32[]{:S(2)}, u32[]{:S(2)}) async-start(f32[8,1,40960]{2,1,0:T(1,128)} %reshape.149), calls=%async_computation | async-start | bytes 2621440 | tf_op jit(solution)/shard_map/all_to_all | solution.py:21
  22.6 173.5 %all-reduce.7.cloned.1.call-start = ((), (), s32[]{:S(2)}) async-start(), calls=%async_computation.2 | async-start | bytes 2097152 | tf_op jit(solution)/shard_map/psum | solution.py:14
  23.7 413.8 %all-reduce.5.cloned.1.call-start = ((), (), s32[]{:S(2)}) async-start(), calls=%async_computation.1 | async-start | bytes 41943040 | tf_op jit(solution)/shard_map/psum | solution.py:14
  437.5 5.8 %copy-start.14 = (f32[64,5120]{1,0:T(8,128)S(1)}, f32[64,5120]{1,0:T(8,128)}, u32[]{:S(2)}) copy-start(f32[64,5120]{1,0:T(8,128)} %get-tuple-element.6) | copy-start | bytes 3932164
  437.5 5.8 %copy-start.22 = (f32[256,128]{1,0:T(8,128)S(1)}, f32[256,128]{1,0:T(8,128)}, u32[]{:S(2)}) copy-start(f32[256,128]{1,0:T(8,128)} %get-tuple-element.21) | copy-start | bytes 393220
  443.3 4.4 copy-start.13
  443.3 4.4 copy-start.21
  447.7 4.6 copy-start.12
  452.3 4.4 copy-start.11
  452.3 4.4 copy-start.20
  456.7 4.3 copy-start.10
  461.1 4.8 copy-start.9
  461.1 4.8 copy-start.19
  465.9 4.3 copy-start.8
  470.2 4.4 copy-start.7
  470.3 4.4 copy-start.18
  474.7 4.5 copy-start.6
  479.2 4.4 copy-start.5
  479.2 4.4 copy-start.17
  483.6 4.3 copy-start.4
  488.0 4.6 copy-start.3
  488.0 4.6 copy-start.16
  492.6 4.3 copy-start.2
  497.0 4.4 copy-start.1
  497.0 4.4 copy-start.15
  501.4 4.6 copy-start
Sparse Core Ops, SparseCore 0:
  26.5 89.0 all-reduce.6
  196.1 241.2 all-reduce.4
where the time goes:
time: 526 us; the launch traced here: 519 us
  waiting for transfers between devices  259 us (49%)
  local copies, waits for them, and re-layouts  142 us (27%)
  matrix products  74.1 us (14%)
  other arithmetic  20.4 us (4%)
  between operations  14.6 us (3%)
  starting transfers between devices  8.53 us (2%)
    psum x2, waiting for transfers between devices, broadcast(): return lax.psum(block, axis)  241 us
    select_n x64, local copies, waits for them, and re-layouts, broadcast(): jnp.where(lax.axis_index(axis) == holder, block, jnp.zeros_like(block))  132 us
    dot_general x16, matrix products, per_device(): jnp.dot(left_piece[:, left_offset:left_offset + unit], right_piece, preci...  74.1 us
    all_to_all x1, waiting for transfers between devices, per_device(): lax.all_to_all(blocks, 'col', split_axis=1, concat_axis=2, tiled=True)  17.9 us
    select_n x2, other arithmetic, broadcast(): jnp.where(lax.axis_index(axis) == holder, block, jnp.zeros_like(block))  15.1 us
  transfers between devices with their start and end apart: 3, of which 2 were waited for; matrix products, arithmetic and copies ran while one was open for 30% of the time, Pallas kernels for 0%

commit v1 on v0

v1 whole, which is shorter than its diff:
```python
import jax
import jax.numpy as jnp
import numpy as np
from jax import lax
from jax.experimental import pallas as pl
from jax.experimental.pallas import tpu as pltpu
from jax.sharding import PartitionSpec as P

MESH = pl.DeviceIdType.MESH
F32, BF16 = jnp.float32, jnp.bfloat16
O, V, K = 64, 640, 1024
COLS = 5120
CHUNKS = 8
W = COLS // CHUNKS
W4 = 256
W1 = W - W4
GROUPS = COLS // 512


def cols_of(n, first=0, width=W):
    return pl.ds(pl.multiple_of(n * W + first, 128), width)


def rows_of(start, count):
    return pl.ds(pl.multiple_of(start, 8), count)


def regroup(x_ref, tmp, stage, groups):
    low = lax.broadcasted_iota(jnp.int32, (8, 128), 1) < 64

    @pl.loop(0, 8)
    def _(q):
        for slot, g in enumerate(groups):
            for t in range(4):
                v = x_ref[rows_of(q * 80 + g * 8, 8), t * 128 : (t + 1) * 128]
                nxt = pltpu.roll(v, 7, 0)
                tmp[slot, 2 * t] = jnp.where(low, v, pltpu.roll(nxt, 64, 1))
                tmp[slot, 2 * t + 1] = jnp.where(low, pltpu.roll(v, 64, 1), nxt)
            for u in range(4):
                at = (g * 4 + u) * 128
                stage[rows_of(q * 8, 8), at : at + 128] = tmp[slot, :, 2 * u, :]


def kernel(a_ref, x_ref, perm_ref, o_ref, b, stage, tmp, ag, al, c_buf,
           p1, in1, t4y, t1y, t4f, t1f, in4, sib, asem, ssem, assem, csem, osem):
    r, q = lax.axis_index("row"), lax.axis_index("col")
    xlo, y, core = r // 8, (r // 2) % 4, r % 2
    z, xhi = q // 2, q % 2
    side = (xlo + xhi) % 2

    def dev(xlo, y, core, z, xhi):
        return (xlo * 8 + y * 2 + core, z * 2 + xhi)

    def block(y):
        return core * 512 + y * 128

    yp, ym, y2 = (y + 1) % 4, (y + 3) % 4, (y + 2) % 4
    up, down = dev(xlo, yp, core, z, xhi), dev(xlo, ym, core, z, xhi)
    inner = dev(1 - xlo, y, core, z, xhi)
    sibling = dev(xlo, y, 1 - core, z, xhi)
    far = dev(xlo, y, core, z, 1 - xhi)
    mates = []
    for dz in range(4):
        for dx in range(2):
            if dz or dx:
                oz, ox = (z + dz) % 4, (xhi + dx) % 2
                mates.append((oz * 2 + ox, dev((side + ox) % 2, y, core, oz, ox)))
    zmates = [dev(xlo, y, core, (z + d) % 4, xhi) for d in (1, 2, 3)]
    mine = block(y) + side * 64
    other = (1 - side) * 64

    barrier = pltpu.get_barrier_semaphore()
    greeted = [m for _, m in mates] + [up, down, inner, sibling, far]
    for d in greeted:
        pl.semaphore_signal(barrier, inc=1, device_id=d, device_id_type=MESH)
    regroup(x_ref, tmp, stage, (0, 1))
    pl.semaphore_wait(barrier, len(greeted))

    def push(n, row, count, cols, to, recv):
        ref = b.at[rows_of(row, count), cols]
        pltpu.make_async_remote_copy(
            src_ref=ref, dst_ref=ref, send_sem=ssem.at[n], recv_sem=recv, device_id=to, device_id_type=MESH
        ).start()

    def arrived(row, count, cols, recv):
        ref = b.at[rows_of(row, count), cols]
        pltpu.make_async_copy(ref, ref, recv).wait()

    def exchange(n):
        for oq, d in mates:
            pltpu.make_async_remote_copy(
                src_ref=stage.at[rows_of(oq * 8, 8), cols_of(n)],
                dst_ref=b.at[rows_of(mine + q * 8, 8), cols_of(n)],
                send_sem=ssem.at[n], recv_sem=p1.at[n], device_id=d, device_id_type=MESH,
            ).start()

    def a_push(src, slot, to, i):
        return pltpu.make_async_remote_copy(
            src_ref=src, dst_ref=ag.at[slot], send_sem=assem.at[i], recv_sem=asem.at[i],
            device_id=to, device_id_type=MESH,
        )

    fq = z * 2 + 1 - xhi

    def a_copies():
        first = [a_push(a_ref, q, far, 0)] + [a_push(a_ref, q, d, 1 + i) for i, d in enumerate(zmates)]
        second = [a_push(ag.at[fq], fq, d, 4 + i) for i, d in enumerate(zmates)]
        return first, second

    def a_arrived(slot, i):
        pltpu.make_async_copy(ag.at[slot], ag.at[slot], asem.at[i]).wait()

    exchange(0)
    regroup(x_ref, tmp, stage, (2, 3, 4))
    exchange(1)
    own = pltpu.make_async_copy(stage.at[rows_of(q * 8, 8)], b.at[rows_of(mine + q * 8, 8)], osem)
    regroup(x_ref, tmp, stage, (5, 6, 7, 8, 9))
    own.start()
    own.wait()

    @pl.loop(0, CHUNKS + 4)
    def _(i):
        @pl.when(i < CHUNKS)
        def _():
            n = i
            c4, c1 = cols_of(n, 0, W4), cols_of(n, W4, W1)
            arrived(0, 56, cols_of(n), p1.at[n])
            push(n, mine, 64, c1, inner, in1.at[n])
            push(n, mine, 64, c4, up, t4y.at[n, 0])
            push(n, mine, 64, c4, down, t4y.at[n, 1])
            push(n, mine, 64, c4, inner, in4.at[n, 0])

        @pl.when(i < CHUNKS - 2)
        def _():
            exchange(i + 2)

        @pl.when(i == 0)
        def _():
            for c in a_copies()[0]:
                c.start()

        @pl.when(jnp.logical_and(i >= 1, i < CHUNKS + 1))
        def _():
            n = i - 1
            c4, c1 = cols_of(n, 0, W4), cols_of(n, W4, W1)
            arrived(block(y) + other, 64, c1, in1.at[n])
            push(n, block(y), 128, c1, up, t1y.at[n, 0])
            push(n, block(y), 128, c1, down, t1y.at[n, 1])
            arrived(block(ym) + side * 64, 64, c4, t4y.at[n, 0])
            push(n, block(ym) + side * 64, 32, c4, up, t4f.at[n, 0])
            push(n, block(ym) + side * 64, 64, c4, inner, in4.at[n, 1])
            arrived(block(yp) + side * 64, 64, c4, t4y.at[n, 1])
            push(n, block(yp) + side * 64 + 32, 32, c4, down, t4f.at[n, 1])
            push(n, block(yp) + side * 64, 64, c4, inner, in4.at[n, 2])

        @pl.when(i == 1)
        def _():
            a_arrived(fq, 0)
            for c in a_copies()[1]:
                c.start()

        @pl.when(jnp.logical_and(i >= 2, i < CHUNKS + 2))
        def _():
            n = i - 2
            c4, c1 = cols_of(n, 0, W4), cols_of(n, W4, W1)
            arrived(block(ym), 128, c1, t1y.at[n, 0])
            push(n, block(ym), 64, c1, up, t1f.at[n, 0])
            arrived(block(yp), 128, c1, t1y.at[n, 1])
            push(n, block(yp) + 64, 64, c1, down, t1f.at[n, 1])
            arrived(block(y2) + side * 64, 32, c4, t4f.at[n, 0])
            arrived(block(y2) + side * 64 + 32, 32, c4, t4f.at[n, 1])
            push(n, block(y2) + side * 64, 64, c4, inner, in4.at[n, 3])
            for j, yy in enumerate((y, ym, yp)):
                arrived(block(yy) + other, 64, c4, in4.at[n, j])
                push(n, block(yy), 128, cols_of(n), sibling, sib.at[n, j])

        @pl.when(jnp.logical_and(i >= 3, i < CHUNKS + 3))
        def _():
            n = i - 3
            c4, c1 = cols_of(n, 0, W4), cols_of(n, W4, W1)
            arrived(block(y2), 64, c1, t1f.at[n, 0])
            arrived(block(y2) + 64, 64, c1, t1f.at[n, 1])
            arrived(block(y2) + other, 64, c4, in4.at[n, 3])
            push(n, block(y2), 128, cols_of(n), sibling, sib.at[n, 3])

        @pl.when(i == 3)
        def _():
            for j in range(3):
                d = 3 - j
                a_arrived(((z + d) % 4) * 2 + xhi, 1 + j)
                a_arrived(((z + d) % 4) * 2 + 1 - xhi, 4 + j)
            ag[q] = a_ref[...]
            for yy in range(4):
                t = jnp.concatenate([ag[yy], ag[4 + yy]], axis=1)
                hi = t.astype(BF16)
                lo = (t - hi.astype(F32)).astype(BF16)
                both = jnp.dot(jnp.concatenate([hi, lo], axis=0), perm_ref[...], preferred_element_type=F32)
                both = both.astype(BF16)
                for c in range(2):
                    al[:, c * 512 + yy * 128 : c * 512 + yy * 128 + 128] = both[:, c * 128 : c * 128 + 128]

        @pl.when(i >= 4)
        def _():
            n = i - 4
            for j, yy in enumerate((y, ym, yp, y2)):
                arrived((1 - core) * 512 + yy * 128, 128, cols_of(n), sib.at[n, j])
            for at, width in ((0, 256), (256, 256), (512, 128)):
                t = b[:, cols_of(n, at, width)]
                hi = t.astype(BF16)
                lo = (t - hi.astype(F32)).astype(BF16)
                one = jnp.dot(al[...], hi, preferred_element_type=F32)
                two = jnp.dot(al[0:256], lo, preferred_element_type=F32)
                c_buf[:, cols_of(n, at, width)] = one[0:256] + (one[256:512] + two)
            pltpu.make_async_copy(c_buf.at[:, cols_of(n)], o_ref.at[:, cols_of(n)], csem.at[n]).start()

    @pl.loop(0, CHUNKS)
    def _(n):
        pltpu.make_async_copy(c_buf.at[:, cols_of(n)], o_ref.at[:, cols_of(n)], csem.at[n]).wait()
        sent = b.at[0:1016, cols_of(n)]
        pltpu.make_async_copy(sent, sent, ssem.at[n]).wait()

    for group in a_copies():
        for c in group:
            c.wait_send()


def permutation():
    perm = np.zeros((256, 256), np.float32)
    for o in range(256):
        core, side, s, k8 = o // 128, (o // 64) % 2, (o // 8) % 8, o % 8
        perm[((side + s) % 2) * 128 + core * 64 + s * 8 + k8, o] = 1
    return perm


def per_device(integrals, amplitudes):
    vmem = pl.BlockSpec(memory_space=pltpu.VMEM)
    dma = pltpu.SemaphoreType.DMA
    return pl.pallas_call(
        kernel,
        name="cycle",
        out_shape=jax.ShapeDtypeStruct((256, COLS), F32),
        in_specs=[vmem, vmem, vmem],
        out_specs=pl.BlockSpec(memory_space=pl.ANY),
        scratch_shapes=[
            pltpu.VMEM((K, COLS), F32),
            pltpu.VMEM((64, COLS), F32),
            pltpu.VMEM((5, 8, 8, 128), F32),
            pltpu.VMEM((8, 256, 128), F32),
            pltpu.VMEM((512, K), BF16),
            pltpu.VMEM((256, COLS), F32),
            dma((CHUNKS,)),
            dma((CHUNKS,)),
            dma((CHUNKS, 2)),
            dma((CHUNKS, 2)),
            dma((CHUNKS, 2)),
            dma((CHUNKS, 2)),
            dma((CHUNKS, 4)),
            dma((CHUNKS, 4)),
            dma((7,)),
            dma((CHUNKS,)),
            dma((7,)),
            dma((CHUNKS,)),
            dma(()),
        ],
        compiler_params=pltpu.CompilerParams(collective_id=0, has_side_effects=True, vmem_limit_bytes=50 << 20),
        cost_estimate=pl.CostEstimate(flops=3 * 2 * 256 * K * COLS, bytes_accessed=7 << 20, transcendentals=0),
    )(integrals, amplitudes, jnp.asarray(permutation(), BF16))


def solution(mesh):
    placed = (P("row", "col"), P("row", "col"))
    return jax.shard_map(
        per_device, mesh=mesh, in_specs=placed, out_specs=P("row", "col"), check_vma=False
    )
```

time: 526 us -> 98.4 us (0.19); the launches traced: 519 us -> 98.2 us
  waiting for transfers between devices: 259 us -> 0 us
  local copies, waits for them, and re-layouts: 142 us -> 8.53 us
  Pallas kernels: 0 us -> 89.7 us
  matrix products: 74.1 us -> 0 us
  other arithmetic: 20.4 us -> 0 us
  between operations: 14.6 us -> 0.01 us
  starting transfers between devices: 8.53 us -> 0 us
    psum x2 -> x0, waiting for transfers between devices: 241 us -> none  [broadcast(): return lax.psum(block, axis)]
    select_n x64 -> x0, local copies, waits for them, and re-layouts: 132 us -> none  [broadcast(): jnp.where(lax.axis_index(axis) == holder, block, jnp.zeros_like(block))]
    pallas_call x0 -> x1, Pallas kernels: none -> 89.7 us  [per_device(): pl.pallas_call(kernel, name='cycle', out_shape=jax.ShapeDtypeStruct((256,...]
    dot_general x16 -> x0, matrix products: 74.1 us -> none  [per_device(): jnp.dot(left_piece[:, left_offset:left_offset + unit], right_piece, preci...]
    all_to_all x1 -> x0, waiting for transfers between devices: 17.9 us -> none  [per_device(): lax.all_to_all(blocks, 'col', split_axis=1, concat_axis=2, tiled=True)]
    select_n x2 -> x0, other arithmetic: 15.1 us -> none  [broadcast(): jnp.where(lax.axis_index(axis) == holder, block, jnp.zeros_like(block))]
    all_to_all x1 -> x0, starting transfers between devices: 8.45 us -> none  [per_device(): lax.all_to_all(blocks, 'col', split_axis=1, concat_axis=2, tiled=True)]
  transfers between devices with their start and end apart: 3 -> 0, of which waited for: 2 -> 0; matrix products, arithmetic and copies ran while one was open for 30% -> 0% of each run, Pallas kernels for 0% -> 0%
where the time goes in v1:
time: 98.4 us; the launch traced here: 98.2 us
  Pallas kernels  89.7 us (91%)
  local copies, waits for them, and re-layouts  8.53 us (9%)
    pallas_call x1, Pallas kernels, per_device(): pl.pallas_call(kernel, name='cycle', out_shape=jax.ShapeDtypeStruct((256,...  89.7 us
    unnamed x7, local copies, waits for them, and re-layouts  8.53 us

profile of v1, /device:TPU:1, one launch (start us, length us, event | category | flops | bytes accessed | tf_op | source)
XLA Modules:
  0.0 98.2 jit_solution(8553835771735175345)
XLA Ops:
  0.0 0.0 copy-start
  0.0 1.3 %copy-done = f32[640,512]{1,0:T(8,128)S(1)} copy-done((f32[640,512]{1,0:T(8,128)S(1)}, f32[640,512]{1,0:T(8,128)}, u32[]{:S(2)}) %copy-start) | copy-done | bytes 1310744
  1.3 0.0 copy-start.1
  1.3 0.9 copy-done.1
  2.2 0.0 copy-start.2
  2.2 0.9 copy-done.2
  3.1 89.7 %cycle.1 = f32[256,5120]{1,0:T(8,128)} custom-call(f32[256,128]{1,0:T(8,128)S(1)} %copy-done.1, f32[640,512]{1,0:T(8,128)S(1)} %copy-done, bf16[256,256]{1,0:T(8,128)(2,1)S(1)} %copy-done.2), custom_call_target="tpu_custom_call" | custom-call | flops 8053063680 | bytes 7340032 | tf_op jit(solution)/shard_map/cycle/pallas_call | solution.py:238
  92.8 5.4 %copy.5 = f32[256,5120]{1,0:T(8,128)} copy(f32[256,5120]{1,0:T(8,128)} %cycle.1) | data formatting | bytes 10485760
Async XLA Ops:
  0.0 1.3 %copy-start = (f32[640,512]{1,0:T(8,128)S(1)}, f32[640,512]{1,0:T(8,128)}, u32[]{:S(2)}) copy-start(f32[640,512]{1,0:T(8,128)} %x_ref.1) | copy-start | bytes 3932164
  1.3 0.9 copy-start.1
  2.2 0.9 copy-start.2

commit v2 on v0

v2 whole, which is shorter than its diff:
```python
import jax
import jax.numpy as jnp
from jax import lax
from jax.experimental import pallas as pl
from jax.experimental.pallas import tpu as pltpu
from jax.sharding import PartitionSpec as P

MESH = pl.DeviceIdType.MESH
F32, BF16 = jnp.float32, jnp.bfloat16
COLS = 5120
W = 256
PAIRED = 6
FULL = (COLS - 2 * PAIRED * W) // W
N = PAIRED + FULL
HALF = PAIRED * W
GROUPS = ((0, 1, -2), (1, 2, -1), (3, 3, 0), (6, 4, 4), (10, 4, 7))
A_PAIR, A_OWN, A_NEXT = 2, 5, 2
LAG2, LAG3, LAGC, LAGO = 2, 4, 6, 9


def at(start, size, unit):
    return pl.ds(pl.multiple_of(start, unit), size)


def regroup(x_ref, tmp, stage, groups):
    low = lax.broadcasted_iota(jnp.int32, (8, 128), 1) < 64

    @pl.loop(0, 8)
    def _(q):
        for slot, g in enumerate(groups):
            for t in range(4):
                v = x_ref[at(q * 80 + g * 8, 8, 8), t * 128 : (t + 1) * 128]
                nxt = pltpu.roll(v, 7, 0)
                tmp[slot, 2 * t] = jnp.where(low, v, pltpu.roll(nxt, 64, 1))
                tmp[slot, 2 * t + 1] = jnp.where(low, pltpu.roll(v, 64, 1), nxt)
            for u in range(4):
                col = (g * 4 + u) * 128
                stage[at(q * 8, 8, 8), col : col + 128] = tmp[slot, :, 2 * u, :]


def permutation(xlo, z, xhi):
    i = lax.broadcasted_iota(jnp.int32, (256, 256), 0)
    o = lax.broadcasted_iota(jnp.int32, (256, 256), 1)
    from_xlo = (xlo + (o >> 6)) & 1
    from_z = (z + 4 - ((o >> 4) & 3)) & 3
    from_xhi = (xhi + (o >> 3)) & 1
    source = from_xlo * 128 + ((o >> 7) & 1) * 64 + from_z * 16 + from_xhi * 8 + (o & 7)
    return (i == source).astype(F32).astype(BF16)


def kernel(a_in, x_in, o_ref, b, stage, tmp, ag, al, c_out, x_ref,
           ex, exs, ty, tf, sib, cr, ssem, cs, ar, asend, lsem):
    r, q = lax.axis_index("row"), lax.axis_index("col")
    xlo, y, core = r // 8, (r // 2) % 4, r % 2
    z, xhi = q // 2, q % 2

    def dev(xlo, y, core, z, xhi):
        return (xlo * 8 + y * 2 + core, z * 2 + xhi)

    up, down = dev(xlo, (y + 1) % 4, core, z, xhi), dev(xlo, (y + 3) % 4, core, z, xhi)
    inner = dev(1 - xlo, y, core, z, xhi)
    outer = dev(1 - xlo, y, core, z, 1 - xhi)
    sibling = dev(xlo, y, 1 - core, z, xhi)
    plane = []
    for d in range(1, 16):
        oxlo, oz, oxhi = (xlo + d // 8) % 2, (z + (d // 2) % 4) % 4, (xhi + d % 2) % 2
        plane.append((d, oxlo, oz * 2 + oxhi, dev(oxlo, y, core, oz, oxhi)))
    z_up, z_down = dev(xlo, y, core, (z + 1) % 4, xhi), dev(xlo, y, core, (z + 3) % 4, xhi)

    load_x = pltpu.make_async_copy(x_in, x_ref, lsem.at[0])
    load_a = pltpu.make_async_copy(a_in, ag.at[0, q], lsem.at[1])
    load_x.start()
    load_a.start()
    barrier = pltpu.get_barrier_semaphore()
    greeted = [p[3] for p in plane] + [up, down, sibling]
    for d in greeted:
        pl.semaphore_signal(barrier, inc=1, device_id=d, device_id_type=MESH)
    load_x.wait()
    regroup(x_ref, tmp, stage, (0, HALF // 512))
    pl.semaphore_wait(barrier, len(greeted))

    def cols(n):
        return at(n * W, W, W)

    def push(n, src, dst, count, to, recv):
        pltpu.make_async_remote_copy(
            src_ref=b.at[at(src, count, 8), cols(n)], dst_ref=b.at[at(dst, count, 8), cols(n)],
            send_sem=ssem.at[n], recv_sem=recv, device_id=to, device_id_type=MESH,
        ).start()

    def arrived(n, row, count, recv):
        ref = b.at[at(row, count, 8), cols(n)]
        pltpu.make_async_copy(ref, ref, recv).wait()

    def mine(slot):
        return slot * 256 + core * 128

    def exchange(g):
        n, count, _ = GROUPS[g]
        for d, oxlo, oq, to in plane:
            first = at(oxlo * HALF + n * W, count * W, W) if n < PAIRED else pl.ds(HALF + n * W, count * W)
            pltpu.make_async_remote_copy(
                src_ref=stage.at[at(oq * 8, 8, 8), first],
                dst_ref=b.at[at(mine(0) + d * 8, 8, 8), pl.ds(n * W, count * W)],
                send_sem=exs.at[g], recv_sem=ex.at[g], device_id=to, device_id_type=MESH,
            ).start()

    def exchanged(g, sem):
        n, count, _ = GROUPS[g]
        ref = b.at[at(mine(0) + 8, 120, 8), pl.ds(n * W, count * W)]
        pltpu.make_async_copy(ref, ref, sem.at[g]).wait()

    def own_piece():
        rows, into = at(q * 8, 8, 8), at(mine(0), 8, 8)
        return [
            pltpu.make_async_copy(stage.at[rows, at(xlo * HALF, HALF, W)], b.at[into, 0:HALF], lsem.at[2]),
            pltpu.make_async_copy(stage.at[rows, 2 * HALF : COLS], b.at[into, HALF : N * W], lsem.at[3]),
        ]

    def a_push(rows, block, to_rows, i, to, part=pl.ds(0, 256)):
        return pltpu.make_async_remote_copy(
            src_ref=ag.at[rows, block, part], dst_ref=ag.at[to_rows, block, part],
            send_sem=asend.at[i], recv_sem=ar.at[i], device_id=to, device_id_type=MESH,
        )

    def a_arrived(rows, block, i, part=pl.ds(0, 256)):
        ref = ag.at[rows, block, part]
        pltpu.make_async_copy(ref, ref, ar.at[i]).wait()

    qo = z * 2 + 1 - xhi
    a_x = lambda: [a_push(0, q, 1, 0, inner), a_push(0, q, 1, 1, outer)]
    a_far = lambda: [a_push(1, q, 0, 2, outer)]
    top, bottom = pl.ds(0, 128), pl.ds(128, 128)

    def a_block(step, j):
        return ((z + step) % 4) * 2 + (xhi if j == 0 else 1 - xhi)

    def a_z(rows, i):
        return [
            a_push(rows, a_block(0, j), rows, i + 2 * j + k, to) for j in range(2) for k, to in enumerate((z_up, z_down))
        ]

    def a_z_next(rows, i):
        return [
            a_push(rows, a_block(3, j), rows, i + 4 + 2 * j, z_up, top) for j in range(2)
        ] + [
            a_push(rows, a_block(1, j), rows, i + 5 + 2 * j, z_down, bottom) for j in range(2)
        ]

    def a_z_arrived(rows, i):
        for j in range(2):
            a_arrived(rows, a_block(3, j), i + 2 * j)
            a_arrived(rows, a_block(1, j), i + 2 * j + 1)

    def a_z_all(rows, i):
        for j in range(2):
            a_arrived(rows, a_block(2, j), i + 4 + 2 * j, top)
            a_arrived(rows, a_block(2, j), i + 5 + 2 * j, bottom)

    def a_split(rows):
        perm = permutation(xlo, z, xhi)
        for slot, step in enumerate((0, 3, 1, 2)):
            yy = (y + step) % 4
            t = jnp.concatenate([ag[rows, yy], ag[rows, 4 + yy]], axis=1)
            hi = t.astype(BF16)
            lo = (t - hi.astype(F32)).astype(BF16)
            both = jnp.dot(jnp.concatenate([hi, lo], axis=0), perm, preferred_element_type=F32)
            al[rows, :, slot * 256 : slot * 256 + 256] = both.astype(BF16)

    def product(rows, n, first, depth):
        t = b[first : first + depth, cols(n)]
        hi = t.astype(BF16)
        lo = (t - hi.astype(F32)).astype(BF16)
        one = jnp.dot(al[rows, :, first : first + depth], hi, preferred_element_type=F32)
        two = jnp.dot(al[rows, 0:256, first : first + depth], lo, preferred_element_type=F32)
        return one[0:256] + (one[256:512] + two)

    def all_here(n, slots):
        for slot in slots:
            arrived(n, slot * 256 + (1 - core) * 128, 128, sib.at[n, slot])

    def c_copy(n):
        return pltpu.make_async_remote_copy(
            src_ref=c_out.at[n], dst_ref=o_ref.at[:, at(xlo * HALF + n * W, W, W)],
            send_sem=cs.at[n], recv_sem=cr.at[n], device_id=inner, device_id_type=MESH,
        )

    exchange(0)
    load_a.wait()
    for c in a_x():
        c.start()
    regroup(x_ref, tmp, stage, (1, 2, HALF // 512 + 1, HALF // 512 + 2))
    exchange(1)
    regroup(x_ref, tmp, stage, tuple(range(2 * HALF // 512, COLS // 512)))
    pieces = own_piece()
    for c in pieces:
        c.start()
    for c in pieces:
        c.wait()

    def when(*conditions):
        ok = conditions[0]
        for c in conditions[1:]:
            ok = jnp.logical_and(ok, c)
        return pl.when(ok)

    @pl.loop(0, N + LAGC)
    def _(i):
        for g, (first, _, start) in enumerate(GROUPS):
            if start >= 0:
                @when(i == start)
                def _(g=g):
                    exchange(g)

            @when(i == first)
            def _(g=g):
                exchanged(g, ex)

        @when(i < N)
        def _():
            n = i
            push(n, mine(0), 256 + core * 128, 128, up, ty.at[n, 0])
            push(n, mine(0), 512 + core * 128, 128, down, ty.at[n, 1])

        @when(i == A_PAIR)
        def _():
            a_arrived(1, q, 0)
            a_arrived(1, qo, 1)
            for c in a_z(1, 3) + a_far():
                c.start()

        @when(i == A_OWN)
        def _():
            a_arrived(0, qo, 2)
            for c in a_z(0, 11):
                c.start()

        @when(i == A_PAIR + A_NEXT)
        def _():
            a_z_arrived(1, 3)
            for c in a_z_next(1, 3):
                c.start()

        @when(i == A_OWN + A_NEXT)
        def _():
            a_z_arrived(0, 11)
            for c in a_z_next(0, 11):
                c.start()

        @when(i >= LAG2, i < N + LAG2)
        def _():
            n = i - LAG2
            arrived(n, mine(1), 128, ty.at[n, 0])
            push(n, mine(1), mine(3), 64, up, tf.at[n, 0])
            arrived(n, mine(2), 128, ty.at[n, 1])
            push(n, mine(2) + 64, mine(3) + 64, 64, down, tf.at[n, 1])
            for slot in range(3):
                push(n, mine(slot), mine(slot), 128, sibling, sib.at[n, slot])

        @when(i >= LAG3, i < N + LAG3)
        def _():
            n = i - LAG3
            arrived(n, mine(3), 64, tf.at[n, 0])
            arrived(n, mine(3) + 64, 64, tf.at[n, 1])
            push(n, mine(3), mine(3), 128, sibling, sib.at[n, 3])

        @when(i == LAGC)
        def _():
            a_z_all(1, 3)
            a_split(1)

        @when(i >= LAGC, i < LAGC + PAIRED)
        def _():
            n = i - LAGC
            all_here(n, range(4))
            c_out[n] = product(1, n, 0, 1024)
            c_copy(n).start()

        @when(i == LAGO)
        def _():
            a_z_all(0, 11)
            a_split(0)

        @when(i >= LAGO, i < LAGO + PAIRED)
        def _():
            n = i - LAGO
            o_ref[:, at(xlo * HALF + n * W, W, W)] = product(0, n, 0, 1024)

        @when(i >= LAGC + PAIRED)
        def _():
            n = i - LAGC
            all_here(n, range(3))
            part = product(0, n, 0, 768)
            all_here(n, (3,))
            o_ref[:, at(HALF + n * W, W, W)] = part + product(0, n, 768, 256)

    @pl.loop(0, PAIRED)
    def _(n):
        c = pltpu.make_async_copy(c_out.at[n], o_ref.at[:, at((1 - xlo) * HALF + n * W, W, W)], cr.at[n])
        c.wait()
        pltpu.make_async_copy(c_out.at[n], c_out.at[n], cs.at[n]).wait()

    @pl.loop(0, N)
    def _(n):
        sent = b.at[0:896, cols(n)]
        pltpu.make_async_copy(sent, sent, ssem.at[n]).wait()

    for g in range(len(GROUPS)):
        exchanged(g, exs)
    for c in a_x() + a_far() + a_z(1, 3) + a_z(0, 11) + a_z_next(1, 3) + a_z_next(0, 11):
        c.wait_send()


def write(c_ref, o_ref, sem):
    parts = [(c_ref.at[pl.ds(32 * i, 32)], o_ref.at[pl.ds(32 * i, 32)], sem.at[i]) for i in range(8)]
    for part in parts:
        pltpu.make_async_copy(*part).start()
    for part in parts:
        pltpu.make_async_copy(*part).wait()


def per_device(integrals, amplitudes):
    dma = pltpu.SemaphoreType.DMA
    anywhere = pl.BlockSpec(memory_space=pl.ANY)
    c = pl.pallas_call(
        kernel,
        name="cycle",
        out_shape=pltpu.VMEM((256, COLS), F32),
        in_specs=[anywhere, anywhere],
        out_specs=pl.BlockSpec(memory_space=pltpu.VMEM),
        scratch_shapes=[
            pltpu.VMEM((1024, N * W), F32),
            pltpu.VMEM((64, COLS), F32),
            pltpu.VMEM((4, 8, 8, 128), F32),
            pltpu.VMEM((2, 8, 256, 128), F32),
            pltpu.VMEM((2, 512, 1024), BF16),
            pltpu.VMEM((PAIRED, 256, W), F32),
            pltpu.VMEM((640, 512), F32),
            dma((len(GROUPS),)),
            dma((len(GROUPS),)),
            dma((N, 2)),
            dma((N, 2)),
            dma((N, 4)),
            dma((PAIRED,)),
            dma((N,)),
            dma((PAIRED,)),
            dma((19,)),
            dma((19,)),
            dma((4,)),
        ],
        compiler_params=pltpu.CompilerParams(collective_id=0, has_side_effects=True, vmem_limit_bytes=52 << 20),
        cost_estimate=pl.CostEstimate(flops=3 * 2 * 256 * 1024 * COLS, bytes_accessed=7 << 20, transcendentals=0),
    )(integrals, amplitudes)
    return pl.pallas_call(
        write,
        name="write",
        out_shape=jax.ShapeDtypeStruct((256, COLS), F32),
        in_specs=[pl.BlockSpec(memory_space=pltpu.VMEM)],
        out_specs=anywhere,
        scratch_shapes=[dma((8,))],
        compiler_params=pltpu.CompilerParams(vmem_limit_bytes=8 << 20),
    )(c)


def solution(mesh):
    placed = (P("row", "col"), P("row", "col"))
    return jax.shard_map(
        per_device, mesh=mesh, in_specs=placed, out_specs=P("row", "col"), check_vma=False
    )
```

time: 526 us -> 84 us (0.16); the launches traced: 519 us -> 83.2 us
  waiting for transfers between devices: 259 us -> 0 us
  local copies, waits for them, and re-layouts: 142 us -> 0 us
  Pallas kernels: 0 us -> 83.2 us
  matrix products: 74.1 us -> 0 us
  other arithmetic: 20.4 us -> 0 us
  between operations: 14.6 us -> 0.01 us
  starting transfers between devices: 8.53 us -> 0 us
    psum x2 -> x0, waiting for transfers between devices: 241 us -> none  [broadcast(): return lax.psum(block, axis)]
    select_n x64 -> x0, local copies, waits for them, and re-layouts: 132 us -> none  [broadcast(): jnp.where(lax.axis_index(axis) == holder, block, jnp.zeros_like(block))]
    pallas_call x0 -> x2, Pallas kernels: none -> 83.2 us  [the longest x1 80.7 us: per_device(): pl.pallas_call(kernel, name='cycle', out_shape=pltpu.VMEM((256, COLS), F3...]
    dot_general x16 -> x0, matrix products: 74.1 us -> none  [per_device(): jnp.dot(left_piece[:, left_offset:left_offset + unit], right_piece, preci...]
    all_to_all x1 -> x0, waiting for transfers between devices: 17.9 us -> none  [per_device(): lax.all_to_all(blocks, 'col', split_axis=1, concat_axis=2, tiled=True)]
    select_n x2 -> x0, other arithmetic: 15.1 us -> none  [broadcast(): jnp.where(lax.axis_index(axis) == holder, block, jnp.zeros_like(block))]
    all_to_all x1 -> x0, starting transfers between devices: 8.45 us -> none  [per_device(): lax.all_to_all(blocks, 'col', split_axis=1, concat_axis=2, tiled=True)]
    unnamed x51 -> x0, local copies, waits for them, and re-layouts: 7.74 us -> none
  transfers between devices with their start and end apart: 3 -> 0, of which waited for: 2 -> 0; matrix products, arithmetic and copies ran while one was open for 30% -> 0% of each run, Pallas kernels for 0% -> 0%
where the time goes in v2:
time: 84 us; the launch traced here: 83.2 us
  Pallas kernels  83.2 us (99%)
    pallas_call x1, Pallas kernels, per_device(): pl.pallas_call(kernel, name='cycle', out_shape=pltpu.VMEM((256, COLS), F3...  80.7 us
    pallas_call x1, Pallas kernels, per_device(): pl.pallas_call(write, name='write', out_shape=jax.ShapeDtypeStruct((256,...  2.42 us

profile of v2, /device:TPU:1, one launch (start us, length us, event | category | flops | bytes accessed | tf_op | source)
XLA Modules:
  0.0 83.2 jit_solution(9444572651354188590)
XLA Ops:
  0.0 80.7 %cycle.1.c_ref = f32[256,5120]{1,0:T(8,128)S(1)} custom-call(f32[256,128]{1,0:T(8,128)} %a_in.1, f32[640,512]{1,0:T(8,128)} %x_in.1), custom_call_target="tpu_custom_call" | custom-call | flops 8053063680 | bytes 7340032 | tf_op jit(solution)/shard_map/cycle/pallas_call | solution.py:325
  80.8 2.4 %write.1 = f32[256,5120]{1,0:T(8,128)} custom-call(f32[256,5120]{1,0:T(8,128)S(1)} %cycle.1.c_ref), custom_call_target="tpu_custom_call" | custom-call | tf_op jit(solution)/shard_map/write/pallas_call | solution.py:354

commit v3 on v2

--- a/solution.py
+++ b/solution.py
@@ -22,14 +22,22 @@
     return pl.ds(pl.multiple_of(start, unit), size)
 
 
-def regroup(x_ref, tmp, stage, groups):
+def load(x_in, x_ref, lsem, g):
+    rows = pl.ds(g * 8, 8)
+    return pltpu.make_async_copy(x_in.at[:, rows], x_ref.at[:, rows], lsem.at[g])
+
+
+def regroup(x_in, x_ref, lsem, tmp, stage, groups, first_q=0, count=8, wait=True):
     low = lax.broadcasted_iota(jnp.int32, (8, 128), 1) < 64
-
-    @pl.loop(0, 8)
-    def _(q):
+    for g in groups if wait else ():
+        load(x_in, x_ref, lsem, g).wait()
+
+    @pl.loop(0, count)
+    def _(i):
+        q = (first_q + i) % 8
         for slot, g in enumerate(groups):
             for t in range(4):
-                v = x_ref[at(q * 80 + g * 8, 8, 8), t * 128 : (t + 1) * 128]
+                v = x_ref[q, g * 8 : g * 8 + 8, t * 128 : (t + 1) * 128]
                 nxt = pltpu.roll(v, 7, 0)
                 tmp[slot, 2 * t] = jnp.where(low, v, pltpu.roll(nxt, 64, 1))
                 tmp[slot, 2 * t + 1] = jnp.where(low, pltpu.roll(v, 64, 1), nxt)
@@ -49,7 +57,7 @@
 
 
 def kernel(a_in, x_in, o_ref, b, stage, tmp, ag, al, c_out, x_ref,
-           ex, exs, ty, tf, sib, cr, ssem, cs, ar, asend, lsem):
+           ex, exs, ty, tf, sib, cr, ssem, cs, ar, asend, lsem, oy, oys):
     r, q = lax.axis_index("row"), lax.axis_index("col")
     xlo, y, core = r // 8, (r // 2) % 4, r % 2
     z, xhi = q // 2, q % 2
@@ -67,16 +75,17 @@
         plane.append((d, oxlo, oz * 2 + oxhi, dev(oxlo, y, core, oz, oxhi)))
     z_up, z_down = dev(xlo, y, core, (z + 1) % 4, xhi), dev(xlo, y, core, (z + 3) % 4, xhi)
 
-    load_x = pltpu.make_async_copy(x_in, x_ref, lsem.at[0])
-    load_a = pltpu.make_async_copy(a_in, ag.at[0, q], lsem.at[1])
-    load_x.start()
+    first = (0, HALF // 512)
+    rest = tuple(g for g in range(COLS // 512) if g not in first)
+    for g in first + rest:
+        load(x_in, x_ref, lsem, g).start()
+    load_a = pltpu.make_async_copy(a_in, ag.at[0, q], lsem.at[10])
     load_a.start()
     barrier = pltpu.get_barrier_semaphore()
     greeted = [p[3] for p in plane] + [up, down, sibling]
     for d in greeted:
         pl.semaphore_signal(barrier, inc=1, device_id=d, device_id_type=MESH)
-    load_x.wait()
-    regroup(x_ref, tmp, stage, (0, HALF // 512))
+    regroup(x_in, x_ref, lsem, tmp, stage, first)
     pl.semaphore_wait(barrier, len(greeted))
 
     def cols(n):
@@ -110,12 +119,30 @@
         ref = b.at[at(mine(0) + 8, 120, 8), pl.ds(n * W, count * W)]
         pltpu.make_async_copy(ref, ref, sem.at[g]).wait()
 
+    parts = ((at(xlo * HALF, HALF, 128), pl.ds(0, HALF)), (pl.ds(2 * HALF, FULL * W), pl.ds(HALF, FULL * W)))
+
     def own_piece():
-        rows, into = at(q * 8, 8, 8), at(mine(0), 8, 8)
+        src = at(q * 8, 8, 8)
         return [
-            pltpu.make_async_copy(stage.at[rows, at(xlo * HALF, HALF, W)], b.at[into, 0:HALF], lsem.at[2]),
-            pltpu.make_async_copy(stage.at[rows, 2 * HALF : COLS], b.at[into, HALF : N * W], lsem.at[3]),
+            pltpu.make_async_copy(stage.at[src, frm], b.at[at(mine(0), 8, 8), to], lsem.at[11 + j])
+            for j, (frm, to) in enumerate(parts)
         ]
+
+    def own_along_y():
+        src = at(q * 8, 8, 8)
+        return [
+            pltpu.make_async_remote_copy(
+                src_ref=stage.at[src, frm], dst_ref=b.at[at(mine(1 + k), 8, 8), to],
+                send_sem=oys.at[2 * j + k], recv_sem=oy.at[2 * j + k], device_id=d, device_id_type=MESH,
+            )
+            for j, (frm, to) in enumerate(parts) for k, d in enumerate((up, down))
+        ]
+
+    def own_arrived():
+        for j, (_, to) in enumerate(parts):
+            for k in range(2):
+                ref = b.at[at(mine(1 + k), 8, 8), to]
+                pltpu.make_async_copy(ref, ref, oy.at[2 * j + k]).wait()
 
     def a_push(rows, block, to_rows, i, to, part=pl.ds(0, 256)):
         return pltpu.make_async_remote_copy(
@@ -186,15 +213,17 @@
         )
 
     exchange(0)
+    regroup(x_in, x_ref, lsem, tmp, stage, rest[:4], q, 1)
+    regroup(x_in, x_ref, lsem, tmp, stage, rest[4:], q, 1)
+    pieces = own_piece()
+    for c in own_along_y() + pieces:
+        c.start()
     load_a.wait()
     for c in a_x():
         c.start()
-    regroup(x_ref, tmp, stage, (1, 2, HALF // 512 + 1, HALF // 512 + 2))
+    regroup(x_in, x_ref, lsem, tmp, stage, rest[:4], q + 1, 7, False)
     exchange(1)
-    regroup(x_ref, tmp, stage, tuple(range(2 * HALF // 512, COLS // 512)))
-    pieces = own_piece()
-    for c in pieces:
-        c.start()
+    regroup(x_in, x_ref, lsem, tmp, stage, rest[4:], q + 1, 7, False)
     for c in pieces:
         c.wait()
 
@@ -219,8 +248,8 @@
         @when(i < N)
         def _():
             n = i
-            push(n, mine(0), 256 + core * 128, 128, up, ty.at[n, 0])
-            push(n, mine(0), 512 + core * 128, 128, down, ty.at[n, 1])
+            push(n, mine(0) + 8, mine(1) + 8, 120, up, ty.at[n, 0])
+            push(n, mine(0) + 8, mine(2) + 8, 120, down, ty.at[n, 1])
 
         @when(i == A_PAIR)
         def _():
@@ -247,12 +276,16 @@
             for c in a_z_next(0, 11):
                 c.start()
 
+        @when(i == LAG2)
+        def _():
+            own_arrived()
+
         @when(i >= LAG2, i < N + LAG2)
         def _():
             n = i - LAG2
-            arrived(n, mine(1), 128, ty.at[n, 0])
+            arrived(n, mine(1) + 8, 120, ty.at[n, 0])
             push(n, mine(1), mine(3), 64, up, tf.at[n, 0])
-            arrived(n, mine(2), 128, ty.at[n, 1])
+            arrived(n, mine(2) + 8, 120, ty.at[n, 1])
             push(n, mine(2) + 64, mine(3) + 64, 64, down, tf.at[n, 1])
             for slot in range(3):
                 push(n, mine(slot), mine(slot), 128, sibling, sib.at[n, slot])
@@ -302,17 +335,19 @@
 
     @pl.loop(0, N)
     def _(n):
-        sent = b.at[0:896, cols(n)]
+        sent = b.at[0:880, cols(n)]
         pltpu.make_async_copy(sent, sent, ssem.at[n]).wait()
 
     for g in range(len(GROUPS)):
         exchanged(g, exs)
+    for c in own_along_y():
+        c.wait_send()
     for c in a_x() + a_far() + a_z(1, 3) + a_z(0, 11) + a_z_next(1, 3) + a_z_next(0, 11):
         c.wait_send()
 
 
 def write(c_ref, o_ref, sem):
-    parts = [(c_ref.at[pl.ds(32 * i, 32)], o_ref.at[pl.ds(32 * i, 32)], sem.at[i]) for i in range(8)]
+    parts = [(c_ref.at[pl.ds(64 * i, 64)], o_ref.at[pl.ds(64 * i, 64)], sem.at[i]) for i in range(4)]
     for part in parts:
         pltpu.make_async_copy(*part).start()
     for part in parts:
@@ -331,11 +366,11 @@
         scratch_shapes=[
             pltpu.VMEM((1024, N * W), F32),
             pltpu.VMEM((64, COLS), F32),
-            pltpu.VMEM((4, 8, 8, 128), F32),
+            pltpu.VMEM((5, 8, 8, 128), F32),
             pltpu.VMEM((2, 8, 256, 128), F32),
             pltpu.VMEM((2, 512, 1024), BF16),
             pltpu.VMEM((PAIRED, 256, W), F32),
-            pltpu.VMEM((640, 512), F32),
+            pltpu.VMEM((8, 80, 512), F32),
             dma((len(GROUPS),)),
             dma((len(GROUPS),)),
             dma((N, 2)),
@@ -346,18 +381,20 @@
             dma((PAIRED,)),
             dma((19,)),
             dma((19,)),
+            dma((13,)),
+            dma((4,)),
             dma((4,)),
         ],
         compiler_params=pltpu.CompilerParams(collective_id=0, has_side_effects=True, vmem_limit_bytes=52 << 20),
         cost_estimate=pl.CostEstimate(flops=3 * 2 * 256 * 1024 * COLS, bytes_accessed=7 << 20, transcendentals=0),
-    )(integrals, amplitudes)
+    )(integrals, amplitudes.reshape(8, 80, 512))
     return pl.pallas_call(
         write,
         name="write",
         out_shape=jax.ShapeDtypeStruct((256, COLS), F32),
         in_specs=[pl.BlockSpec(memory_space=pltpu.VMEM)],
         out_specs=anywhere,
-        scratch_shapes=[dma((8,))],
+        scratch_shapes=[dma((4,))],
         compiler_params=pltpu.CompilerParams(vmem_limit_bytes=8 << 20),
     )(c)
 

time: 84 us -> 82.2 us (0.979)
  Pallas kernels: 83.2 us -> 81.4 us
    pallas_call x1, Pallas kernels: 80.7 us -> 79 us  [per_device(): pl.pallas_call(kernel, name='cycle', out_shape=pltpu.VMEM((256, COLS), F3...]
where the time goes in v3:
time: 82.2 us; the launch traced here: 81.4 us
  Pallas kernels  81.4 us (99%)
    pallas_call x1, Pallas kernels, per_device(): pl.pallas_call(kernel, name='cycle', out_shape=pltpu.VMEM((256, COLS), F3...  79 us
    pallas_call x1, Pallas kernels, per_device(): pl.pallas_call(write, name='write', out_shape=jax.ShapeDtypeStruct((256,...  2.39 us

profile of v3, /device:TPU:1, one launch (start us, length us, event | category | flops | bytes accessed | tf_op | source)
XLA Modules:
  0.0 81.4 jit_solution(11625595711437777837)
XLA Ops:
  0.0 79.0 %cycle.1.c_ref = f32[256,5120]{1,0:T(8,128)S(1)} custom-call(f32[256,128]{1,0:T(8,128)} %a_in.1, f32[8,80,512]{2,1,0:T(8,128)} %bitcast.1), custom_call_target="tpu_custom_call" | custom-call | flops 8053063680 | bytes 7340032 | tf_op jit(solution)/shard_map/cycle/pallas_call | solution.py:360
  79.0 2.4 %write.1 = f32[256,5120]{1,0:T(8,128)} custom-call(f32[256,5120]{1,0:T(8,128)S(1)} %cycle.1.c_ref), custom_call_target="tpu_custom_call" | custom-call | tf_op jit(solution)/shard_map/write/pallas_call | solution.py:391

commit v4 on v3

--- a/solution.py
+++ b/solution.py
@@ -13,9 +13,10 @@
 FULL = (COLS - 2 * PAIRED * W) // W
 N = PAIRED + FULL
 HALF = PAIRED * W
-GROUPS = ((0, 1, -2), (1, 2, -1), (3, 3, 0), (6, 4, 4), (10, 4, 7))
+GROUPS = ((0, 1, -2), (1, 1, -1), (2, 2, 0), (4, 2, 1), (6, 4, 4), (10, 4, 7))
 A_PAIR, A_OWN, A_NEXT = 2, 5, 2
-LAG2, LAG3, LAGC, LAGO = 2, 4, 6, 9
+FAR_FIRST = sorted(range(1, 16), key=lambda d: -(min(d // 2 % 4, 4 - d // 2 % 4) + (0, 2, 1, 1)[d // 8 * 2 + d % 2]))
+LAG2, LAG3, LAGC, LAGO, LAGF = 2, 4, 6, 9, 5
 
 
 def at(start, size, unit):
@@ -70,7 +71,7 @@
     outer = dev(1 - xlo, y, core, z, 1 - xhi)
     sibling = dev(xlo, y, 1 - core, z, xhi)
     plane = []
-    for d in range(1, 16):
+    for d in FAR_FIRST:
         oxlo, oz, oxhi = (xlo + d // 8) % 2, (z + (d // 2) % 4) % 4, (xhi + d % 2) % 2
         plane.append((d, oxlo, oz * 2 + oxhi, dev(oxlo, y, core, oz, oxhi)))
     z_up, z_down = dev(xlo, y, core, (z + 1) % 4, xhi), dev(xlo, y, core, (z + 3) % 4, xhi)
@@ -233,7 +234,7 @@
             ok = jnp.logical_and(ok, c)
         return pl.when(ok)
 
-    @pl.loop(0, N + LAGC)
+    @pl.loop(0, N + LAGF)
     def _(i):
         for g, (first, _, start) in enumerate(GROUPS):
             if start >= 0:
@@ -290,42 +291,42 @@
             for slot in range(3):
                 push(n, mine(slot), mine(slot), 128, sibling, sib.at[n, slot])
 
+        @when(i == LAGC)
+        def _():
+            a_z_all(1, 3)
+            a_split(1)
+
+        @when(i >= LAGC, i < LAGC + PAIRED)
+        def _():
+            n = i - LAGC
+            all_here(n, range(4))
+            c_out[n] = product(1, n, 0, 1024)
+            c_copy(n).start()
+
+        @when(i == LAGO)
+        def _():
+            a_z_all(0, 11)
+            a_split(0)
+
+        @when(i >= LAGO, i < LAGO + PAIRED)
+        def _():
+            n = i - LAGO
+            o_ref[:, at(xlo * HALF + n * W, W, W)] = product(0, n, 0, 1024)
+
+        @when(i >= LAGF + PAIRED)
+        def _():
+            n = i - LAGF
+            all_here(n, range(3))
+            part = product(0, n, 0, 768)
+            all_here(n, (3,))
+            o_ref[:, at(HALF + n * W, W, W)] = part + product(0, n, 768, 256)
+
         @when(i >= LAG3, i < N + LAG3)
         def _():
             n = i - LAG3
             arrived(n, mine(3), 64, tf.at[n, 0])
             arrived(n, mine(3) + 64, 64, tf.at[n, 1])
             push(n, mine(3), mine(3), 128, sibling, sib.at[n, 3])
-
-        @when(i == LAGC)
-        def _():
-            a_z_all(1, 3)
-            a_split(1)
-
-        @when(i >= LAGC, i < LAGC + PAIRED)
-        def _():
-            n = i - LAGC
-            all_here(n, range(4))
-            c_out[n] = product(1, n, 0, 1024)
-            c_copy(n).start()
-
-        @when(i == LAGO)
-        def _():
-            a_z_all(0, 11)
-            a_split(0)
-
-        @when(i >= LAGO, i < LAGO + PAIRED)
-        def _():
-            n = i - LAGO
-            o_ref[:, at(xlo * HALF + n * W, W, W)] = product(0, n, 0, 1024)
-
-        @when(i >= LAGC + PAIRED)
-        def _():
-            n = i - LAGC
-            all_here(n, range(3))
-            part = product(0, n, 0, 768)
-            all_here(n, (3,))
-            o_ref[:, at(HALF + n * W, W, W)] = part + product(0, n, 768, 256)
 
     @pl.loop(0, PAIRED)
     def _(n):

time: 82.2 us -> 81 us (0.985)
  no operation moved by 1% of the time
where the time goes in v4:
time: 81 us; the launch traced here: 80.9 us
  Pallas kernels  80.9 us (100%)
    pallas_call x1, Pallas kernels, per_device(): pl.pallas_call(kernel, name='cycle', out_shape=pltpu.VMEM((256, COLS), F3...  78.5 us
    pallas_call x1, Pallas kernels, per_device(): pl.pallas_call(write, name='write', out_shape=jax.ShapeDtypeStruct((256,...  2.39 us

profile of v4, /device:TPU:1, one launch (start us, length us, event | category | flops | bytes accessed | tf_op | source)
XLA Modules:
  0.0 80.9 jit_solution(15312095245947683294)
XLA Ops:
  0.0 78.5 %cycle.1.c_ref = f32[256,5120]{1,0:T(8,128)S(1)} custom-call(f32[256,128]{1,0:T(8,128)} %a_in.1, f32[8,80,512]{2,1,0:T(8,128)} %bitcast.1), custom_call_target="tpu_custom_call" | custom-call | flops 8053063680 | bytes 7340032 | tf_op jit(solution)/shard_map/cycle/pallas_call | solution.py:361
  78.5 2.4 %write.1 = f32[256,5120]{1,0:T(8,128)} custom-call(f32[256,5120]{1,0:T(8,128)S(1)} %cycle.1.c_ref), custom_call_target="tpu_custom_call" | custom-call | tf_op jit(solution)/shard_map/write/pallas_call | solution.py:392

commit v5 on v4

--- a/solution.py
+++ b/solution.py
@@ -13,7 +13,7 @@
 FULL = (COLS - 2 * PAIRED * W) // W
 N = PAIRED + FULL
 HALF = PAIRED * W
-GROUPS = ((0, 1, -2), (1, 1, -1), (2, 2, 0), (4, 2, 1), (6, 4, 4), (10, 4, 7))
+GROUPS = ((0, 1, -2), (1, 1, -1), (2, 2, 0), (4, 2, 1), (6, 2, 4), (8, 2, 5), (10, 2, 7), (12, 2, 8))
 A_PAIR, A_OWN, A_NEXT = 2, 5, 2
 FAR_FIRST = sorted(range(1, 16), key=lambda d: -(min(d // 2 % 4, 4 - d // 2 % 4) + (0, 2, 1, 1)[d // 8 * 2 + d % 2]))
 LAG2, LAG3, LAGC, LAGO, LAGF = 2, 4, 6, 9, 5

time: 81 us -> 80.8 us (level)
  no operation moved by 1% of the time
where the time goes in v5:
time: 80.8 us; the launch traced here: 80.7 us
  Pallas kernels  80.7 us (100%)
    pallas_call x1, Pallas kernels, per_device(): pl.pallas_call(kernel, name='cycle', out_shape=pltpu.VMEM((256, COLS), F3...  78.3 us
    pallas_call x1, Pallas kernels, per_device(): pl.pallas_call(write, name='write', out_shape=jax.ShapeDtypeStruct((256,...  2.39 us

profile of v5, /device:TPU:1, one launch (start us, length us, event | category | flops | bytes accessed | tf_op | source)
XLA Modules:
  0.0 80.7 jit_solution(10635961076552443872)
XLA Ops:
  0.0 78.3 %cycle.1.c_ref = f32[256,5120]{1,0:T(8,128)S(1)} custom-call(f32[256,128]{1,0:T(8,128)} %a_in.1, f32[8,80,512]{2,1,0:T(8,128)} %bitcast.1), custom_call_target="tpu_custom_call" | custom-call | flops 8053063680 | bytes 7340032 | tf_op jit(solution)/shard_map/cycle/pallas_call | solution.py:361
  78.3 2.4 %write.1 = f32[256,5120]{1,0:T(8,128)} custom-call(f32[256,5120]{1,0:T(8,128)S(1)} %cycle.1.c_ref), custom_call_target="tpu_custom_call" | custom-call | tf_op jit(solution)/shard_map/write/pallas_call | solution.py:392

commit v6 on v5

--- a/solution.py
+++ b/solution.py
@@ -251,6 +251,7 @@
             n = i
             push(n, mine(0) + 8, mine(1) + 8, 120, up, ty.at[n, 0])
             push(n, mine(0) + 8, mine(2) + 8, 120, down, ty.at[n, 1])
+            push(n, mine(0), mine(0), 128, sibling, sib.at[n, 0])
 
         @when(i == A_PAIR)
         def _():
@@ -288,7 +289,7 @@
             push(n, mine(1), mine(3), 64, up, tf.at[n, 0])
             arrived(n, mine(2) + 8, 120, ty.at[n, 1])
             push(n, mine(2) + 64, mine(3) + 64, 64, down, tf.at[n, 1])
-            for slot in range(3):
+            for slot in (1, 2):
                 push(n, mine(slot), mine(slot), 128, sibling, sib.at[n, slot])
 
         @when(i == LAGC)

time: 80.8 us -> 80.8 us (level)
  no operation moved by 1% of the time
where the time goes in v6:
time: 80.8 us; the launch traced here: 80.7 us
  Pallas kernels  80.7 us (100%)
    pallas_call x1, Pallas kernels, per_device(): pl.pallas_call(kernel, name='cycle', out_shape=pltpu.VMEM((256, COLS), F3...  78.3 us
    pallas_call x1, Pallas kernels, per_device(): pl.pallas_call(write, name='write', out_shape=jax.ShapeDtypeStruct((256,...  2.39 us

profile of v6, /device:TPU:1, one launch (start us, length us, event | category | flops | bytes accessed | tf_op | source)
XLA Modules:
  0.0 80.7 jit_solution(11937513009218834368)
XLA Ops:
  0.0 78.3 %cycle.1.c_ref = f32[256,5120]{1,0:T(8,128)S(1)} custom-call(f32[256,128]{1,0:T(8,128)} %a_in.1, f32[8,80,512]{2,1,0:T(8,128)} %bitcast.1), custom_call_target="tpu_custom_call" | custom-call | flops 8053063680 | bytes 7340032 | tf_op jit(solution)/shard_map/cycle/pallas_call | solution.py:362
  78.3 2.4 %write.1 = f32[256,5120]{1,0:T(8,128)} custom-call(f32[256,5120]{1,0:T(8,128)S(1)} %cycle.1.c_ref), custom_call_target="tpu_custom_call" | custom-call | tf_op jit(solution)/shard_map/write/pallas_call | solution.py:393
